TPU v7x, 32 devices: a whole 2x2x4 slice. The times are simulated.
32 devices in a mesh: depth: 16 (over z, y, core), strip: 2 (over x).
Axes of the slice: x: 2, y: 2, z: 4, core: 2. Of those that a mesh axis runs over, the one named last changes fastest.
Arguments:
- sources: bfloat16 [16, 2, 2, 1024, 128], P('depth', 'strip'), may hold values from -6 to 6
- down_state: bfloat16 [16, 2, 2, 1024, 128], P('depth', 'strip'), may hold values from -6 to 6
- up_state: bfloat16 [16, 2, 2, 1024, 128], P('depth', 'strip'), may hold values from -6 to 6
- transfer_op: bfloat16 [16, 2, 2, 1024, 1024], P('depth', 'strip'), may hold values from -0.125 to 0.125
- join_op: bfloat16 [16, 2, 2, 1024, 1024], P('depth', 'strip'), may hold values from -0.125 to 0.125
Outputs:
- down_out: bfloat16 [16, 2, 2, 1024, 128], P('depth', 'strip')
- up_out: bfloat16 [16, 2, 2, 1024, 128], P('depth', 'strip')
All inputs are finite; a program needn't handle non-finite values.
Results may differ from a plain program's by a relative error of at most 0.0075.
Values may be sent and summed in bfloat16 or wider, within the bound.
A program may use at most 64 MiB of HBM per device.

v0:
```python
import jax
import jax.numpy as jnp
from jax import lax
from jax.sharding import PartitionSpec as P

TICKS = 2
PAIRS = 2


def shifted(value, axis, steps):
    count = lax.axis_size(axis)
    leading, last = (max(0, -steps), min(count, count - steps))
    return lax.ppermute(value, axis, [(source, source + steps) for source in range(leading, last)])


def swapped(value, axis, apart):
    mask = 2**apart
    pairs = [(source, source ^ mask) for source in range(lax.axis_size(axis))]
    return lax.ppermute(value, axis, pairs)


def complex_apply(oper, vec, transposed):
    axis_k = 1 if transposed else 2
    from_re = lax.dot_general(
        oper, vec[0], (((axis_k,), (0,)), ((), ())), preferred_element_type=jnp.float32
    )
    from_im = lax.dot_general(
        oper, vec[1], (((axis_k,), (0,)), ((), ())), preferred_element_type=jnp.float32
    )
    real_part = from_re[0] - from_im[1]
    imag_part = from_re[1] + from_im[0]
    return jnp.stack([real_part, imag_part], axis=0)


def add_round(first, second):
    return (first.astype(jnp.float32) + second.astype(jnp.float32)).astype(jnp.bfloat16)


def finish(a_trace, b_trace, partner_a, partner_b, transfer, joiner):
    joined_a = (a_trace.astype(jnp.float32) + complex_apply(joiner, partner_a, False)).astype(
        jnp.bfloat16
    )
    joined_b = (b_trace.astype(jnp.float32) + complex_apply(joiner, partner_b, True)).astype(
        jnp.bfloat16
    )
    new_down = complex_apply(transfer, joined_a, False).astype(jnp.bfloat16)
    new_up = complex_apply(transfer, joined_b, True).astype(jnp.bfloat16)
    return (new_down, new_up)


def per_device(sources, down_state, up_state, transfer_op, join_op):
    source = sources[0, 0]
    transfer = transfer_op[0, 0]
    joiner = join_op[0, 0]
    down = down_state[0, 0]
    upward = up_state[0, 0]
    for tick in range(TICKS):
        in_down = shifted(down, "depth", PAIRS)
        in_up = shifted(upward, "depth", -PAIRS)
        a_trace = add_round(source, in_down)
        b_trace = add_round(source, in_up)
        partner_a, partner_b = swapped((a_trace, b_trace), "strip", 0)
        down, upward = finish(a_trace, b_trace, partner_a, partner_b, transfer, joiner)
    return (down[None, None], upward[None, None])


def solution(mesh):
    return jax.shard_map(
        per_device,
        mesh=mesh,
        in_specs=(
            P("depth", "strip", None, None, None),
            P("depth", "strip", None, None, None),
            P("depth", "strip", None, None, None),
            P("depth", "strip", None, None, None),
            P("depth", "strip", None, None, None),
        ),
        out_specs=(P("depth", "strip", None, None, None), P("depth", "strip", None, None, None)),
        check_vma=False,
    )
```

profile of v0, /device:TPU:24, one launch (start us, length us, event | category | flops | bytes accessed | tf_op | source)
XLA Modules:
  0.0 120.1 jit_solution(14251403517120425818)
XLA Ops:
  0.6 1.2 %copy.8 = bf16[1,1,2,1024,128]{3,4,2,1,0:T(8,128)(2,1)S(1)} copy(bf16[1,1,2,1024,128]{4,3,2,1,0:T(8,128)(2,1)} %param.6) | data formatting | bytes 1048576 | tf_op args[1]
  1.9 3.4 %collective-permute-start = (bf16[2,1024,128]{1,2,0:T(8,128)(2,1)S(1)}, bf16[2,1024,128]{1,2,0:T(8,128)(2,1)S(1)}, u32[]{:S(2)}, u32[]{:S(2)}) collective-permute-start(bf16[2,1024,128]{1,2,0:T(8,128)(2,1)S(1)} %bitcast.178), channel_id=1, source_target_pairs={{0,4},{2,6},{4,8},{6,10},{8,12},{10,14},{12,16},{14,18},{16,20},{1... | collective-permute-start | bytes 1572872 | tf_op jit(solution)/shard_map/ppermute | solution.py:13
  5.3 1.2 %copy.9 = bf16[1,1,2,1024,128]{3,4,2,1,0:T(8,128)(2,1)S(1)} copy(bf16[1,1,2,1024,128]{4,3,2,1,0:T(8,128)(2,1)} %param.7) | data formatting | bytes 1048576 | tf_op args[2]
  6.6 3.3 %collective-permute-start.4 = (bf16[2,1024,128]{1,2,0:T(8,128)(2,1)S(1)}, bf16[2,1024,128]{1,2,0:T(8,128)(2,1)S(1)}, u32[]{:S(2)}, u32[]{:S(2)}) collective-permute-start(bf16[2,1024,128]{1,2,0:T(8,128)(2,1)S(1)} %bitcast.179), channel_id=1, source_target_pairs={{4,0},{6,2},{8,4},{10,6},{12,8},{14,10},{16,12},{18,14},{20,16},{2... | collective-permute-start | bytes 1572872 | tf_op jit(solution)/shard_map/ppermute | solution.py:13
  9.9 1.2 %copy.7 = bf16[1,1,2,1024,128]{3,4,2,1,0:T(8,128)(2,1)S(1)} copy(bf16[1,1,2,1024,128]{4,3,2,1,0:T(8,128)(2,1)} %param.5) | data formatting | bytes 1048576 | tf_op args[0]
  11.2 7.3 %collective-permute-done = bf16[2,1024,128]{1,2,0:T(8,128)(2,1)S(1)} collective-permute-done((bf16[2,1024,128]{1,2,0:T(8,128)(2,1)S(1)}, bf16[2,1024,128]{1,2,0:T(8,128)(2,1)S(1)}, u32[]{:S(2)}, u32[]{:S(2)}) %collective-permute-start) | collective-permute-done | bytes 524320 | tf_op jit(solution)/shard_map/ppermute | solution.py:13
  18.4 11.1 %collective-permute-done.4 = bf16[2,1024,128]{1,2,0:T(8,128)(2,1)S(1)} collective-permute-done((bf16[2,1024,128]{1,2,0:T(8,128)(2,1)S(1)}, bf16[2,1024,128]{1,2,0:T(8,128)(2,1)S(1)}, u32[]{:S(2)}, u32[]{:S(2)}) %collective-permute-start.4) | collective-permute-done | bytes 524320 | tf_op jit(solution)/shard_map/ppermute | solution.py:13
  29.6 0.3 fusion.82
  29.9 1.6 %collective-permute-start.1 = (bf16[2,1024,128]{1,2,0:T(8,128)(2,1)S(1)}, bf16[2,1024,128]{1,2,0:T(8,128)(2,1)S(1)}, u32[]{:S(2)}, u32[]{:S(2)}) collective-permute-start(bf16[2,1024,128]{1,2,0:T(8,128)(2,1)S(1)} %get-tuple-element.23), channel_id=1, source_target_pairs={{0,1},{1,0},{2,3},{3,2},{4,5},{5,4},{6,7},{7,6},{8,9},{9,8},{10,11... | collective-permute-start | bytes 1572872 | tf_op jit(solution)/shard_map/ppermute | solution.py:19
  31.5 0.5 collective-permute-start.5
  32.0 12.8 %collective-permute-done.1 = bf16[2,1024,128]{1,2,0:T(8,128)(2,1)S(1)} collective-permute-done((bf16[2,1024,128]{1,2,0:T(8,128)(2,1)S(1)}, bf16[2,1024,128]{1,2,0:T(8,128)(2,1)S(1)}, u32[]{:S(2)}, u32[]{:S(2)}) %collective-permute-start.1) | collective-permute-done | bytes 524320 | tf_op jit(solution)/shard_map/ppermute | solution.py:19
  44.8 3.7 %fusion.32 = f32[2,1024,128]{1,2,0:T(8,128)S(1)} fusion(bf16[1,1,2,1024,1024]{4,3,2,1,0:T(8,128)(2,1)} %param.9, bf16[2,1024,128]{1,2,0:T(8,128)(2,1)S(1)} %collective-permute-done.1), kind=kOutput, calls=%fused_computation.36 | convolution fusion | flops 536870912 | bytes 5505024 | tf_op jit(solution)/shard_map/dot_general | solution.py:24
  48.5 1.5 %fusion.35 = f32[2,1024,128]{1,2,0:T(8,128)S(1)} fusion(bf16[1,1,2,1024,1024]{4,3,2,1,0:T(8,128)(2,1)S(1)} %copy-done, bf16[2,1024,128]{1,2,0:T(8,128)(2,1)S(1)} %collective-permute-done.1), kind=kOutput, calls=%fused_computation.37 | convolution fusion | flops 536870912 | bytes 5505024 | tf_op jit(solution)/shard_map/dot_general | solution.py:27
  50.0 0.2 slice_subtract_fusion.7
  50.2 0.2 fusion.84
  50.4 0.3 copy-done.1
  50.7 1.5 %fusion.56 = f32[2,1024,128]{1,2,0:T(8,128)S(1)} fusion(bf16[1,1,2,1024,1024]{4,3,2,1,0:T(8,128)(2,1)S(1)} %copy-done.1, bf16[2,1024,128]{1,2,0:T(8,128)(2,1)S(1)} %fusion.84), kind=kOutput, calls=%fused_computation.44 | convolution fusion | flops 536870912 | bytes 5505024 | tf_op jit(solution)/shard_map/dot_general | solution.py:24
  52.2 1.5 %fusion.59 = f32[2,1024,128]{1,2,0:T(8,128)S(1)} fusion(bf16[1,1,2,1024,1024]{4,3,2,1,0:T(8,128)(2,1)S(1)} %copy-done.1, bf16[2,1024,128]{1,2,0:T(8,128)(2,1)S(1)} %fusion.84), kind=kOutput, calls=%fused_computation.45 | convolution fusion | flops 536870912 | bytes 5505024 | tf_op jit(solution)/shard_map/dot_general | solution.py:27
  53.7 1.3 %collective-permute-done.5 = bf16[2,1024,128]{1,2,0:T(8,128)(2,1)S(1)} collective-permute-done((bf16[2,1024,128]{1,2,0:T(8,128)(2,1)S(1)}, bf16[2,1024,128]{1,2,0:T(8,128)(2,1)S(1)}, u32[]{:S(2)}, u32[]{:S(2)}) %collective-permute-start.5) | collective-permute-done | bytes 524320 | tf_op jit(solution)/shard_map/ppermute | solution.py:19
  55.1 0.7 fusion.44
  55.8 0.7 fusion.47
  56.7 0.2 fusion.86
  56.8 0.7 fusion.68
  57.6 0.7 fusion.71
  58.3 0.2 fusion.95
  58.6 1.9 %collective-permute-start.2 = (bf16[2,1024,128]{1,2,0:T(8,128)(2,1)S(1)}, bf16[2,1024,128]{1,2,0:T(8,128)(2,1)S(1)}, u32[]{:S(2)}, u32[]{:S(2)}) collective-permute-start(bf16[2,1024,128]{1,2,0:T(8,128)(2,1)S(1)} %pad_maximum_fusion), channel_id=1, source_target_pairs={{0,4},{2,6},{4,8},{6,10},{8,12},{10,14},{12,16},{14,18},{16,20},{1... | collective-permute-start | bytes 1572872 | tf_op jit(solution)/shard_map/ppermute | solution.py:13
  60.5 0.2 fusion.91
  60.8 5.0 %collective-permute-start.6 = (bf16[2,1024,128]{1,2,0:T(8,128)(2,1)S(1)}, bf16[2,1024,128]{1,2,0:T(8,128)(2,1)S(1)}, u32[]{:S(2)}, u32[]{:S(2)}) collective-permute-start(bf16[2,1024,128]{1,2,0:T(8,128)(2,1)S(1)} %pad_maximum_fusion.2), channel_id=1, source_target_pairs={{4,0},{6,2},{8,4},{10,6},{12,8},{14,10},{16,12},{18,14},{20,16},{2... | collective-permute-start | bytes 1572872 | tf_op jit(solution)/shard_map/ppermute | solution.py:13
  65.8 8.7 %collective-permute-done.2 = bf16[2,1024,128]{1,2,0:T(8,128)(2,1)S(1)} collective-permute-done((bf16[2,1024,128]{1,2,0:T(8,128)(2,1)S(1)}, bf16[2,1024,128]{1,2,0:T(8,128)(2,1)S(1)}, u32[]{:S(2)}, u32[]{:S(2)}) %collective-permute-start.2) | collective-permute-done | bytes 524320 | tf_op jit(solution)/shard_map/ppermute | solution.py:13
  74.5 11.1 %collective-permute-done.6 = bf16[2,1024,128]{1,2,0:T(8,128)(2,1)S(1)} collective-permute-done((bf16[2,1024,128]{1,2,0:T(8,128)(2,1)S(1)}, bf16[2,1024,128]{1,2,0:T(8,128)(2,1)S(1)}, u32[]{:S(2)}, u32[]{:S(2)}) %collective-permute-start.6) | collective-permute-done | bytes 524320 | tf_op jit(solution)/shard_map/ppermute | solution.py:13
  85.6 0.3 fusion.83
  86.0 1.6 %collective-permute-start.7 = (bf16[2,1024,128]{1,2,0:T(8,128)(2,1)S(1)}, bf16[2,1024,128]{1,2,0:T(8,128)(2,1)S(1)}, u32[]{:S(2)}, u32[]{:S(2)}) collective-permute-start(bf16[2,1024,128]{1,2,0:T(8,128)(2,1)S(1)} %get-tuple-element.20), channel_id=1, source_target_pairs={{0,1},{1,0},{2,3},{3,2},{4,5},{5,4},{6,7},{7,6},{8,9},{9,8},{10,11... | collective-permute-start | bytes 1572872 | tf_op jit(solution)/shard_map/ppermute | solution.py:19
  87.5 0.5 collective-permute-start.3
  88.0 12.8 %collective-permute-done.7 = bf16[2,1024,128]{1,2,0:T(8,128)(2,1)S(1)} collective-permute-done((bf16[2,1024,128]{1,2,0:T(8,128)(2,1)S(1)}, bf16[2,1024,128]{1,2,0:T(8,128)(2,1)S(1)}, u32[]{:S(2)}, u32[]{:S(2)}) %collective-permute-start.7) | collective-permute-done | bytes 524320 | tf_op jit(solution)/shard_map/ppermute | solution.py:19
  100.8 0.7 fusion.50
  101.5 0.7 fusion.53
  102.6 0.7 fusion.74
  103.3 0.7 fusion.77
  104.0 7.1 %collective-permute-done.3 = bf16[2,1024,128]{1,2,0:T(8,128)(2,1)S(1)} collective-permute-done((bf16[2,1024,128]{1,2,0:T(8,128)(2,1)S(1)}, bf16[2,1024,128]{1,2,0:T(8,128)(2,1)S(1)}, u32[]{:S(2)}, u32[]{:S(2)}) %collective-permute-start.3) | collective-permute-done | bytes 524320 | tf_op jit(solution)/shard_map/ppermute | solution.py:19
  111.1 1.5 %fusion.38 = f32[2,1024,128]{1,2,0:T(8,128)S(1)} fusion(bf16[1,1,2,1024,1024]{4,3,2,1,0:T(8,128)(2,1)S(1)} %copy-done, bf16[2,1024,128]{1,2,0:T(8,128)(2,1)S(1)} %collective-permute-done.3), kind=kOutput, calls=%fused_computation.38 | convolution fusion | flops 536870912 | bytes 5505024 | tf_op jit(solution)/shard_map/dot_general | solution.py:24
  112.6 1.5 %fusion.41 = f32[2,1024,128]{1,2,0:T(8,128)S(1)} fusion(bf16[1,1,2,1024,1024]{4,3,2,1,0:T(8,128)(2,1)S(1)} %copy-done, bf16[2,1024,128]{1,2,0:T(8,128)(2,1)S(1)} %collective-permute-done.3), kind=kOutput, calls=%fused_computation.39 | convolution fusion | flops 536870912 | bytes 5505024 | tf_op jit(solution)/shard_map/dot_general | solution.py:27
  114.1 0.2 slice_subtract_fusion.5
  114.5 1.5 %fusion.62 = f32[2,1024,128]{1,2,0:T(8,128)S(1)} fusion(bf16[1,1,2,1024,1024]{4,3,2,1,0:T(8,128)(2,1)S(1)} %copy-done.1, bf16[2,1024,128]{1,2,0:T(8,128)(2,1)S(1)} %fusion.85), kind=kOutput, calls=%fused_computation.46 | convolution fusion | flops 536870912 | bytes 5505024 | tf_op jit(solution)/shard_map/dot_general | solution.py:24
  116.0 1.5 %fusion.65 = f32[2,1024,128]{1,2,0:T(8,128)S(1)} fusion(bf16[1,1,2,1024,1024]{4,3,2,1,0:T(8,128)(2,1)S(1)} %copy-done.1, bf16[2,1024,128]{1,2,0:T(8,128)(2,1)S(1)} %fusion.85), kind=kOutput, calls=%fused_computation.47 | convolution fusion | flops 536870912 | bytes 5505024 | tf_op jit(solution)/shard_map/dot_general | solution.py:27
  117.5 0.2 fusion.98
  117.8 1.0 copy.11
  118.8 0.2 fusion.96
  119.1 1.0 copy.10
  (11 shorter events, 0.8 us)
Async XLA Ops:
  1.9 16.6 %collective-permute-start = (bf16[2,1024,128]{1,2,0:T(8,128)(2,1)S(1)}, bf16[2,1024,128]{1,2,0:T(8,128)(2,1)S(1)}, u32[]{:S(2)}, u32[]{:S(2)}) collective-permute-start(bf16[2,1024,128]{1,2,0:T(8,128)(2,1)S(1)} %bitcast.178), channel_id=1, source_target_pairs={{0,4},{2,6},{4,8},{6,10},{8,12},{10,14},{12,16},{14,18},{16,20},{1... | collective-permute-start | bytes 1572872 | tf_op jit(solution)/shard_map/ppermute | solution.py:13
  6.6 23.0 %collective-permute-start.4 = (bf16[2,1024,128]{1,2,0:T(8,128)(2,1)S(1)}, bf16[2,1024,128]{1,2,0:T(8,128)(2,1)S(1)}, u32[]{:S(2)}, u32[]{:S(2)}) collective-permute-start(bf16[2,1024,128]{1,2,0:T(8,128)(2,1)S(1)} %bitcast.179), channel_id=1, source_target_pairs={{4,0},{6,2},{8,4},{10,6},{12,8},{14,10},{16,12},{18,14},{20,16},{2... | collective-permute-start | bytes 1572872 | tf_op jit(solution)/shard_map/ppermute | solution.py:13
  11.1 37.3 %copy-start = (bf16[1,1,2,1024,1024]{4,3,2,1,0:T(8,128)(2,1)S(1)}, bf16[1,1,2,1024,1024]{4,3,2,1,0:T(8,128)(2,1)}, u32[]{:S(2)}) copy-start(bf16[1,1,2,1024,1024]{4,3,2,1,0:T(8,128)(2,1)} %param.9) | copy-start | bytes 12582916
  29.9 14.8 %collective-permute-start.1 = (bf16[2,1024,128]{1,2,0:T(8,128)(2,1)S(1)}, bf16[2,1024,128]{1,2,0:T(8,128)(2,1)S(1)}, u32[]{:S(2)}, u32[]{:S(2)}) collective-permute-start(bf16[2,1024,128]{1,2,0:T(8,128)(2,1)S(1)} %get-tuple-element.23), channel_id=1, source_target_pairs={{0,1},{1,0},{2,3},{3,2},{4,5},{5,4},{6,7},{7,6},{8,9},{9,8},{10,11... | collective-permute-start | bytes 1572872 | tf_op jit(solution)/shard_map/ppermute | solution.py:19
  31.5 23.6 %collective-permute-start.5 = (bf16[2,1024,128]{1,2,0:T(8,128)(2,1)S(1)}, bf16[2,1024,128]{1,2,0:T(8,128)(2,1)S(1)}, u32[]{:S(2)}, u32[]{:S(2)}) collective-permute-start(bf16[2,1024,128]{1,2,0:T(8,128)(2,1)S(1)} %get-tuple-element.22), channel_id=1, source_target_pairs={{0,1},{1,0},{2,3},{3,2},{4,5},{5,4},{6,7},{7,6},{8,9},{9,8},{10,11... | collective-permute-start | bytes 1572872 | tf_op jit(solution)/shard_map/ppermute | solution.py:19
  48.5 2.2 %copy-start.1 = (bf16[1,1,2,1024,1024]{4,3,2,1,0:T(8,128)(2,1)S(1)}, bf16[1,1,2,1024,1024]{4,3,2,1,0:T(8,128)(2,1)}, u32[]{:S(2)}) copy-start(bf16[1,1,2,1024,1024]{4,3,2,1,0:T(8,128)(2,1)} %param.8) | copy-start | bytes 12582916
  58.6 15.9 %collective-permute-start.2 = (bf16[2,1024,128]{1,2,0:T(8,128)(2,1)S(1)}, bf16[2,1024,128]{1,2,0:T(8,128)(2,1)S(1)}, u32[]{:S(2)}, u32[]{:S(2)}) collective-permute-start(bf16[2,1024,128]{1,2,0:T(8,128)(2,1)S(1)} %pad_maximum_fusion), channel_id=1, source_target_pairs={{0,4},{2,6},{4,8},{6,10},{8,12},{10,14},{12,16},{14,18},{16,20},{1... | collective-permute-start | bytes 1572872 | tf_op jit(solution)/shard_map/ppermute | solution.py:13
  60.8 24.8 %collective-permute-start.6 = (bf16[2,1024,128]{1,2,0:T(8,128)(2,1)S(1)}, bf16[2,1024,128]{1,2,0:T(8,128)(2,1)S(1)}, u32[]{:S(2)}, u32[]{:S(2)}) collective-permute-start(bf16[2,1024,128]{1,2,0:T(8,128)(2,1)S(1)} %pad_maximum_fusion.2), channel_id=1, source_target_pairs={{4,0},{6,2},{8,4},{10,6},{12,8},{14,10},{16,12},{18,14},{20,16},{2... | collective-permute-start | bytes 1572872 | tf_op jit(solution)/shard_map/ppermute | solution.py:13
  86.0 14.8 %collective-permute-start.7 = (bf16[2,1024,128]{1,2,0:T(8,128)(2,1)S(1)}, bf16[2,1024,128]{1,2,0:T(8,128)(2,1)S(1)}, u32[]{:S(2)}, u32[]{:S(2)}) collective-permute-start(bf16[2,1024,128]{1,2,0:T(8,128)(2,1)S(1)} %get-tuple-element.20), channel_id=1, source_target_pairs={{0,1},{1,0},{2,3},{3,2},{4,5},{5,4},{6,7},{7,6},{8,9},{9,8},{10,11... | collective-permute-start | bytes 1572872 | tf_op jit(solution)/shard_map/ppermute | solution.py:19
  87.5 23.6 %collective-permute-start.3 = (bf16[2,1024,128]{1,2,0:T(8,128)(2,1)S(1)}, bf16[2,1024,128]{1,2,0:T(8,128)(2,1)S(1)}, u32[]{:S(2)}, u32[]{:S(2)}) collective-permute-start(bf16[2,1024,128]{1,2,0:T(8,128)(2,1)S(1)} %get-tuple-element.21), channel_id=1, source_target_pairs={{0,1},{1,0},{2,3},{3,2},{4,5},{5,4},{6,7},{7,6},{8,9},{9,8},{10,11... | collective-permute-start | bytes 1572872 | tf_op jit(solution)/shard_map/ppermute | solution.py:19
where the time goes:
time: 120 us
  waiting for transfers between devices  72.2 us (60%)
  matrix products  20.1 us (17%)
  starting transfers between devices  17.8 us (15%)
  local copies, waits for them, and re-layouts  6.08 us (5%)
  other arithmetic  2.93 us (2%)
    ppermute x4, waiting for transfers between devices, shifted(): lax.ppermute(value, axis, [(source, source + steps) for source in range(l...  38.2 us
    ppermute x4, waiting for transfers between devices, swapped(): return lax.ppermute(value, axis, pairs)  33.9 us
    ppermute x4, starting transfers between devices, shifted(): lax.ppermute(value, axis, [(source, source + steps) for source in range(l...  13.7 us
    dot_general x8, matrix products, complex_apply(): lax.dot_general(oper, vec[0], (((axis_k,), (0,)), ((), ())), preferred_el...  11.1 us
    dot_general x8, matrix products, complex_apply(): lax.dot_general(oper, vec[1], (((axis_k,), (0,)), ((), ())), preferred_el...  8.94 us
    unnamed x9, local copies, waits for them, and re-layouts  6.08 us
    ppermute x4, starting transfers between devices, swapped(): return lax.ppermute(value, axis, pairs)  4.18 us
  transfers between devices with their start and end apart: 8, of which 8 were waited for; matrix products, arithmetic and copies ran while one was open for 12% of the time, Pallas kernels for 0%

commit v1 on v0

v1 whole, which is shorter than its diff:
```python
import jax
import jax.numpy as jnp
from jax import lax
from jax.experimental import pallas as pl
from jax.experimental.pallas import tpu as pltpu
from jax.sharding import PartitionSpec as P

TICKS = 2
PAIRS = 2
AHEAD = 4
UP, DOWN = 0, 1


def turned(re, im):
    return -im, re


def kernel(
    src, down, up, t_hbm, j_hbm, down_out, up_out,
    s_v, s_t, j_v, t_v, yr, own, xr, st, acc_u, acc_d, x_u, x_d,
    y_send, y_recv, x_send, x_recv, load_sem, out_sem,
):
    f32, bf16 = jnp.float32, jnp.bfloat16
    m, b = src.shape[-2], src.shape[-1]
    ch = b
    nch = m // ch
    ahead = min(AHEAD, nch // 2)
    wide = 2 * ch
    phases = 2 * TICKS
    layer = lax.axis_index("depth")
    count = lax.axis_size("depth")
    strip = lax.axis_index("strip")
    partner = strip + 1 - 2 * lax.rem(strip, 2)
    has_above = layer >= PAIRS
    has_below = layer < count - PAIRS

    load_s = pltpu.make_async_copy(src.at[0, 0], s_v, load_sem.at[0])
    load_j = pltpu.make_async_copy(j_hbm.at[0, 0], j_v, load_sem.at[1])
    load_t = pltpu.make_async_copy(t_hbm.at[0, 0], t_v, load_sem.at[2])
    load_s.start()

    barrier = pltpu.get_barrier_semaphore()
    pl.semaphore_signal(
        barrier, inc=1, device_id={"strip": partner}, device_id_type=pl.DeviceIdType.MESH
    )

    @pl.when(has_above)
    def _():
        pl.semaphore_signal(
            barrier, inc=1, device_id={"depth": layer - PAIRS},
            device_id_type=pl.DeviceIdType.MESH,
        )

    @pl.when(has_below)
    def _():
        pl.semaphore_signal(
            barrier, inc=1, device_id={"depth": layer + PAIRS},
            device_id_type=pl.DeviceIdType.MESH,
        )

    pl.semaphore_wait(barrier, 1 + has_above.astype(jnp.int32) + has_below.astype(jnp.int32))

    def y_copy(p, j):
        tick, flow = divmod(p, 2)
        if tick == 0:
            state = (up, down)[flow]
            source = state.at[0, 0, :, pl.ds(j * ch, ch), :]
        else:
            source = st.at[p - 2, j]
        to = layer - PAIRS if flow == UP else layer + PAIRS
        return pltpu.make_async_remote_copy(
            src_ref=source, dst_ref=yr.at[p, j],
            send_sem=y_send.at[p, j], recv_sem=y_recv.at[p, j],
            device_id={"depth": to}, device_id_type=pl.DeviceIdType.MESH,
        )

    def y_start(g):
        p, j = divmod(g, nch)
        if p < phases:
            @pl.when((has_above, has_below)[p % 2])
            def _():
                y_copy(p, j).start()

    def x_copy(p, j):
        return pltpu.make_async_remote_copy(
            src_ref=own.at[p, j], dst_ref=xr.at[p, j],
            send_sem=x_send.at[p, j], recv_sem=x_recv.at[p, j],
            device_id={"strip": partner}, device_id_type=pl.DeviceIdType.MESH,
        )

    for g in range(ahead):
        y_start(g)
    load_j.start()
    load_t.start()

    @pl.when(jnp.logical_not(has_below))
    def _():
        for tick in range(TICKS):
            yr[2 * tick + UP] = jnp.zeros(yr.shape[1:], bf16)

    @pl.when(jnp.logical_not(has_above))
    def _():
        for tick in range(TICKS):
            yr[2 * tick + DOWN] = jnp.zeros(yr.shape[1:], bf16)

    load_s.wait()

    def stage(p, j):
        tick, flow = divmod(p, 2)

        @pl.when((has_below, has_above)[flow])
        def _():
            y_copy(p, j).wait_recv()

        rows = slice(j * ch, (j + 1) * ch)
        for c in range(2):
            arrived = yr[p, j, c].astype(f32)
            if flow == UP:
                if tick == 0:
                    source = s_v[c, rows, :].astype(f32).T
                    s_t[j, c] = source.astype(bf16)
                    arrived = arrived.T
                else:
                    source = s_t[j, c].astype(f32)
            else:
                source = s_v[c, rows, :].astype(f32)
            total = (source + arrived).astype(bf16)
            own[p, j, c] = total
        x_copy(p, j).start()

    def join(p, k):
        flow = p % 2
        x_copy(p, 2 * k).wait_recv()
        x_copy(p, 2 * k + 1).wait_recv()
        axis = 1 if flow == UP else 0
        re = jnp.concatenate([xr[p, 2 * k, 0], xr[p, 2 * k + 1, 0]], axis=axis)
        im = jnp.concatenate([xr[p, 2 * k, 1], xr[p, 2 * k + 1, 1]], axis=axis)
        first = jnp.concatenate([re, im], axis=1 - axis)
        second = jnp.concatenate(turned(re, im), axis=1 - axis)
        inner = slice(k * wide, (k + 1) * wide)
        if flow == UP:
            for i in range(m // wide):
                cols = slice(i * wide, (i + 1) * wide)
                part = jnp.dot(
                    first, j_v[0, inner, cols], preferred_element_type=f32
                ) + jnp.dot(second, j_v[1, inner, cols], preferred_element_type=f32)
                acc_u[:, cols] = part if k == 0 else acc_u[:, cols] + part
        else:
            part = jnp.dot(
                j_v[0, :, inner], first, preferred_element_type=f32
            ) + jnp.dot(j_v[1, :, inner], second, preferred_element_type=f32)
            acc_d[...] = part if k == 0 else acc_d[...] + part

    def rounded(p):
        for j in range(nch):
            near = slice(j * ch, (j + 1) * ch)
            for c in range(2):
                far = slice(c * b, (c + 1) * b)
                trace = own[p, j, c].astype(f32)
                other = slice((1 - c) * b, (2 - c) * b)
                if p % 2 == UP:
                    joined = (acc_u[far, near] + trace).astype(bf16)
                    x_u[0, far, near] = joined
                    x_u[1, other, near] = joined if c == 0 else -joined
                else:
                    joined = (acc_d[near, far] + trace).astype(bf16)
                    x_d[0, near, far] = joined
                    x_d[1, near, other] = joined if c == 0 else -joined

    def out_copy(p, j):
        result = (up_out, down_out)[p % 2]
        return pltpu.make_async_copy(
            st.at[p, j], result.at[0, 0, :, pl.ds(j * ch, ch), :], out_sem.at[p % 2, j]
        )

    def transfer(p, i):
        tick, flow = divmod(p, 2)
        part = slice(i * wide, (i + 1) * wide)
        if flow == UP:
            value = jnp.dot(
                x_u[0], t_v[0, :, part], preferred_element_type=f32
            ) + jnp.dot(x_u[1], t_v[1, :, part], preferred_element_type=f32)
        else:
            value = jnp.dot(
                t_v[0, part, :], x_d[0], preferred_element_type=f32
            ) + jnp.dot(t_v[1, part, :], x_d[1], preferred_element_type=f32)
        for h in range(2):
            near = slice(h * ch, (h + 1) * ch)
            for c in range(2):
                far = slice(c * b, (c + 1) * b)
                if flow == UP:
                    piece = value[far, near]
                    if tick == TICKS - 1:
                        piece = piece.T
                else:
                    piece = value[near, far]
                st[p, 2 * i + h, c] = piece.astype(bf16)
            if tick == TICKS - 1:
                out_copy(p, 2 * i + h).start()

    pairs = nch // 2
    lag = 2
    todo = {}

    def at(step, call, *args):
        todo.setdefault(step, []).append((call, args))

    end = phases * nch
    for p in range(phases):
        base = p * nch
        for k in range(pairs):
            at(min(base + 2 * k + 1 + lag, end), join, p, k)
        at(min(base + nch + lag, end), rounded, p)
        for i in range(pairs):
            step = base + 2 * nch - ahead + (i if p == phases - 2 else 2 * i)
            at(min(step, end), transfer, p, i)

    for g in range(end):
        p, j = divmod(g, nch)
        stage(p, j)
        if g == 3:
            load_j.wait()
        if g == nch:
            load_t.wait()
        for call, args in todo.get(g, ()):
            call(*args)
        y_start(g + ahead)
    for call, args in todo.get(end, ()):
        call(*args)

    for p in range(phases):
        for j in range(nch):
            x_copy(p, j).wait_send()

            @pl.when((has_above, has_below)[p % 2])
            def _():
                y_copy(p, j).wait_send()
    for p in (phases - 2, phases - 1):
        for j in range(nch):
            out_copy(p, j).wait()


def per_device(sources, down_state, up_state, transfer_op, join_op):
    m, b = sources.shape[-2:]
    nch = m // b
    phases = 2 * TICKS
    bf16, f32 = jnp.bfloat16, jnp.float32
    out = jax.ShapeDtypeStruct(sources.shape, bf16)
    chunked = (phases, nch, 2, b, b)
    return pl.pallas_call(
        kernel,
        out_shape=(out, out),
        in_specs=[pl.BlockSpec(memory_space=pl.ANY)] * 5,
        out_specs=[pl.BlockSpec(memory_space=pl.ANY)] * 2,
        scratch_shapes=[
            pltpu.VMEM((2, m, b), bf16),
            pltpu.VMEM((nch, 2, b, b), bf16),
            pltpu.VMEM((2, m, m), bf16),
            pltpu.VMEM((2, m, m), bf16),
            pltpu.VMEM(chunked, bf16),
            pltpu.VMEM(chunked, bf16),
            pltpu.VMEM(chunked, bf16),
            pltpu.VMEM(chunked, bf16),
            pltpu.VMEM((2 * b, m), f32),
            pltpu.VMEM((m, 2 * b), f32),
            pltpu.VMEM((2, 2 * b, m), bf16),
            pltpu.VMEM((2, m, 2 * b), bf16),
            pltpu.SemaphoreType.DMA((phases, nch)),
            pltpu.SemaphoreType.DMA((phases, nch)),
            pltpu.SemaphoreType.DMA((phases, nch)),
            pltpu.SemaphoreType.DMA((phases, nch)),
            pltpu.SemaphoreType.DMA((3,)),
            pltpu.SemaphoreType.DMA((2, nch)),
        ],
        compiler_params=pltpu.CompilerParams(
            collective_id=0, has_side_effects=True, vmem_limit_bytes=60 * 1024 * 1024
        ),
        cost_estimate=pl.CostEstimate(
            flops=TICKS * 32 * m * m * b, bytes_accessed=8 * m * (m + 2 * b), transcendentals=0
        ),
    )(sources, down_state, up_state, transfer_op, join_op)


def solution(mesh):
    spec = P("depth", "strip", None, None, None)
    return jax.shard_map(
        per_device,
        mesh=mesh,
        in_specs=(spec,) * 5,
        out_specs=(spec, spec),
        check_vma=False,
    )
```

time: 120 us -> 72.6 us (0.60)
  waiting for transfers between devices: 72.2 us -> 0 us
  Pallas kernels: 0 us -> 67.9 us
  matrix products: 20.1 us -> 0 us
  starting transfers between devices: 17.8 us -> 0 us
  other arithmetic: 2.93 us -> 0 us
  local copies, waits for them, and re-layouts: 6.08 us -> 3.74 us
    ppermute x8 -> x0, waiting for transfers between devices: 72.2 us -> none  [the longest x4 38.2 us: shifted(): lax.ppermute(value, axis, [(source, source + steps) for source in range(l...]
    pallas_call x0 -> x1, Pallas kernels: none -> 67.9 us  [per_device(): pl.pallas_call(kernel, out_shape=(out, out), in_specs=[pl.BlockSpec(memor...]
    dot_general x16 -> x0, matrix products: 20.1 us -> none  [the longest x8 11.1 us: complex_apply(): lax.dot_general(oper, vec[0], (((axis_k,), (0,)), ((), ())), preferred_el...]
    ppermute x8 -> x0, starting transfers between devices: 17.8 us -> none  [the longest x4 13.7 us: shifted(): lax.ppermute(value, axis, [(source, source + steps) for source in range(l...]
    unnamed x9 -> x2, local copies, waits for them, and re-layouts: 6.08 us -> 3.74 us
    convert_element_type x6 -> x0, other arithmetic: 1.3 us -> none  [the longest x2 0.67 us: add_round(): (first.astype(jnp.float32) + second.astype(jnp.float32)).astype(jnp.bfloa...]
  transfers between devices with their start and end apart: 8 -> 0, of which waited for: 8 -> 0; matrix products, arithmetic and copies ran while one was open for 12% -> 0% of each run, Pallas kernels for 0% -> 0%
where the time goes in v1:
time: 72.6 us; the launch traced here: 72.3 us
  Pallas kernels  67.9 us (94%)
  local copies, waits for them, and re-layouts  3.74 us (5%)
    pallas_call x1, Pallas kernels, per_device(): pl.pallas_call(kernel, out_shape=(out, out), in_specs=[pl.BlockSpec(memor...  67.9 us
    unnamed x2, local copies, waits for them, and re-layouts  3.74 us

profile of v1, /device:TPU:24, one launch (start us, length us, event | category | flops | bytes accessed | tf_op | source)
XLA Modules:
  0.0 72.3 jit_solution(9972186760489796891)
XLA Ops:
  0.6 67.9 %shard_map.68 = (bf16[1,1,2,1024,128]{4,3,2,1,0:T(8,128)(2,1)}, bf16[1,1,2,1024,128]{4,3,2,1,0:T(8,128)(2,1)}) custom-call(bf16[1,1,2,1024,128]{4,3,2,1,0:T(8,128)(2,1)} %src.1, bf16[1,1,2,1024,128]{4,3,2,1,0:T(8,128)(2,1)} %down.1, bf16[1,1,2,1024,128]{4,3,2,1,0:T(8,128)(2,1)} %up.1, bf16[1,1,2,1024,1024]{4,3,2,1,0:T(8,128)(2,1)} %t_hbm.1, ...), custom_call_target="tpu_custom_call" | custom-call | flops 8589934592 | bytes 10485760 | tf_op jit(solution)/shard_map/pallas_call | solution.py:250
  68.6 1.9 %copy.9 = bf16[1,1,2,1024,128]{4,3,2,1,0:T(8,128)(2,1)} copy(bf16[1,1,2,1024,128]{4,3,2,1,0:T(8,128)(2,1)} %get-tuple-element.4) | data formatting | bytes 1048576
  70.4 1.9 %copy.10 = bf16[1,1,2,1024,128]{4,3,2,1,0:T(8,128)(2,1)} copy(bf16[1,1,2,1024,128]{4,3,2,1,0:T(8,128)(2,1)} %get-tuple-element.5) | data formatting | bytes 1048576
